TPU v7x, 32 devices: a whole 2x2x4 slice. The times are simulated.
32 devices in a mesh: section: 2 (over core), dp: 4 (over z), seq: 4 (over y, x).
Axes of the slice: x: 2, y: 2, z: 4, core: 2. Of those that a mesh axis runs over, the one named last changes fastest.
Arguments:
- enc_states: bfloat16 [8, 512, 4096], P(('section', 'dp'), 'seq'), may hold values from -6 to 6
- enc_gain: float32 [4096], replicated, may hold values from 0.1 to 1.9
- key_weight: bfloat16 [4096, 4096], P(None, 'seq'), may hold values from -0.09375 to 0.09375
- value_weight: bfloat16 [4096, 4096], P(None, 'seq'), may hold values from -0.09375 to 0.09375
- queries: bfloat16 [8, 512, 4096], P(('section', 'dp'), None, 'seq'), may hold values from -28 to 28
- out_grad: bfloat16 [8, 512, 4096], P(('section', 'dp'), None, 'seq'), may hold values from -6 to 6
- lengths: int32 [8], replicated, may hold values from 256 to 512, as said below
Outputs:
- attended: bfloat16 [8, 512, 4096], P(('section', 'dp'), None, 'seq')
- enc_grad: bfloat16 [8, 512, 4096], P(('section', 'dp'), 'seq')
- key_grad: float32 [4096, 4096], P(('section', 'dp'), 'seq')
- value_grad: float32 [4096, 4096], P(('section', 'dp'), 'seq')
- query_grad: bfloat16 [8, 512, 4096], P(('section', 'dp'), None, 'seq')
Inputs may be any that keep to these rules, and one draw needn't show every extreme that they name: `lengths`: positions at or beyond a sequence's length are padding; at least one sequence in every draw has length 512.
All inputs are finite; a program needn't handle non-finite values.
Results may differ from a plain program's by a relative error of at most 0.023.
The roundings to bfloat16 on the way count: a program that leaves them out, or rounds other values in their place, can miss the bound.
Values may be sent and summed in bfloat16 or wider, within the bound.
No kernel may reach another device: no remote copies, remote signals or barrier semaphores. Data moves between devices by JAX's collectives and lax.ppermute only.
A program may use at most 128 MiB of HBM per device.

v0:
```python
import jax
import jax.numpy as jnp
from jax import lax
from jax.sharding import PartitionSpec as P

HD = 256


EPS = 1e-06
NEG_FILL = -1e30


def partner_2(value, axis, stride):
    mask = 2**stride
    pairs = [(source, source ^ mask) for source in range(lax.axis_size(axis))]
    return lax.ppermute(value, axis, pairs)


def normalize(enc_rows, gain):
    wide_rows = enc_rows.astype(jnp.float32)
    factor = lax.rsqrt(jnp.mean(wide_rows * wide_rows, axis=-1, keepdims=True) + EPS)
    return ((wide_rows * factor * gain).astype(jnp.bfloat16), factor)


def norm_backward(enc_rows, factor, gain, row_grad):
    wide_rows = enc_rows.astype(jnp.float32)
    scaled = row_grad.astype(jnp.float32) * gain
    inner_sum = jnp.mean(scaled * wide_rows, axis=-1, keepdims=True)
    return (factor * scaled - wide_rows * factor * factor * factor * inner_sum).astype(jnp.bfloat16)


def attend(query_rows, key_rows, value_rows, upstream, visible):
    score_scale = HD ** (-0.5)
    scores = (
        jnp.einsum("thd,shd->hts", query_rows, key_rows, preferred_element_type=jnp.float32)
        * score_scale
    )
    scores = jnp.where(visible[None, None, :], scores, NEG_FILL)
    row_max = jnp.max(scores, axis=-1, keepdims=True)
    exponent = jnp.exp(scores - row_max)
    probability = exponent / jnp.sum(exponent, axis=-1, keepdims=True)
    prob_weights = probability.astype(jnp.bfloat16)
    attended = jnp.einsum(
        "hts,shd->thd", prob_weights, value_rows, preferred_element_type=jnp.float32
    ).astype(jnp.bfloat16)
    grad_probs = jnp.einsum(
        "thd,shd->hts", upstream, value_rows, preferred_element_type=jnp.float32
    )
    inner_sum = jnp.sum(probability * grad_probs, axis=-1, keepdims=True)
    grad_scores = (probability * (grad_probs - inner_sum) * score_scale).astype(jnp.bfloat16)
    query_grad = jnp.einsum(
        "hts,shd->thd", grad_scores, key_rows, preferred_element_type=jnp.float32
    ).astype(jnp.bfloat16)
    key_grad = jnp.einsum(
        "hts,thd->shd", grad_scores, query_rows, preferred_element_type=jnp.float32
    ).astype(jnp.bfloat16)
    value_grad = jnp.einsum(
        "hts,thd->shd", prob_weights, upstream, preferred_element_type=jnp.float32
    ).astype(jnp.bfloat16)
    return (attended, query_grad, key_grad, value_grad)


def on_device(enc_states, enc_gain, key_weight, value_weight, queries, out_grad, lengths):
    enc_rows = enc_states[0]
    normed, factor = normalize(enc_rows, enc_gain)
    head_width = key_weight.shape[1]
    heads_here = head_width // HD
    projection = jnp.concatenate([key_weight, value_weight], axis=1)
    dp_count = lax.axis_size("dp")
    batch_count = lax.axis_size("section") * dp_count
    position = lax.axis_index("section") * dp_count + lax.axis_index("dp")
    partner = (position + dp_count) % batch_count
    src_rows = enc_rows.shape[0] * lax.axis_size("seq")
    positions = jnp.arange(src_rows, dtype=jnp.int32)
    target_rows = queries.shape[1]
    visible = positions < lengths[partner]
    partner_rows = partner_2(normed, "section", 0)
    gathered = lax.all_gather(partner_rows, "seq", axis=0, tiled=True)
    keys_values = jnp.dot(gathered, projection, preferred_element_type=jnp.float32).astype(
        jnp.bfloat16
    )
    query_rows = queries[0].reshape(target_rows, heads_here, HD)
    upstream = out_grad[0].reshape(target_rows, heads_here, HD)
    key_rows = keys_values[:, :head_width].reshape(src_rows, heads_here, HD)
    value_rows = keys_values[:, head_width:].reshape(src_rows, heads_here, HD)
    attended, query_grad, key_grad, value_grad = attend(
        query_rows, key_rows, value_rows, upstream, visible
    )
    kv_grads = jnp.concatenate(
        [key_grad.reshape(src_rows, head_width), value_grad.reshape(src_rows, head_width)], axis=1
    )
    attended, query_grad, kv_grads = (
        attended.reshape(target_rows, head_width),
        query_grad.reshape(target_rows, head_width),
        kv_grads,
    )
    row_share = lax.psum_scatter(
        lax.dot_general(
            kv_grads, projection, (((1,), (1,)), ((), ())), preferred_element_type=jnp.float32
        ).astype(jnp.bfloat16),
        "seq",
        scatter_dimension=0,
        tiled=True,
    )
    row_grad = partner_2(row_share, "section", 0)
    weight_term = lax.dot_general(
        gathered, kv_grads, (((0,), (0,)), ((), ())), preferred_element_type=jnp.float32
    )
    summed = lax.psum_scatter(
        weight_term.astype(jnp.bfloat16), ("section", "dp"), scatter_dimension=0, tiled=True
    ).astype(jnp.float32)
    enc_grad = norm_backward(enc_rows, factor, enc_gain, row_grad)
    return (
        attended[None],
        enc_grad[None],
        summed[:, :head_width],
        summed[:, head_width:],
        query_grad[None],
    )


def solution(mesh):
    placed = (
        P(("section", "dp"), "seq", None),
        P(),
        P(None, "seq"),
        P(None, "seq"),
        P(("section", "dp"), None, "seq"),
        P(("section", "dp"), None, "seq"),
        P(),
    )
    return jax.shard_map(
        on_device,
        mesh=mesh,
        in_specs=placed,
        out_specs=(
            P(("section", "dp"), None, "seq"),
            P(("section", "dp"), "seq", None),
            P(("section", "dp"), "seq"),
            P(("section", "dp"), "seq"),
            P(("section", "dp"), None, "seq"),
        ),
        check_vma=False,
    )
```

profile of v0, /device:TPU:0, one launch (start us, length us, event | category | flops | bytes accessed | tf_op | source)
XLA Modules:
  0.0 510.4 jit_solution(15320442823771317866)
XLA Ops:
  7.2 1.7 fusion.16
  8.9 1.6 fusion.11
  10.5 0.5 collective-permute-start
  11.0 2.3 collective-permute-done
  13.3 1.0 copy-done.3
  14.3 0.0 reduce-scatter.3.cloned.1.call-start
  14.3 1.3 copy.32
  15.7 0.5 copy.33
  16.2 0.6 dynamic_slice.3
  16.8 0.6 iota_compare_fusion
  17.5 7.9 %constant_dynamic-update-slice_fusion.1 = bf16[4096,2048]{1,0:T(8,128)(2,1)} fusion(bf16[4096,1024]{1,0:T(8,128)(2,1)} %param.9), kind=kLoop, calls=%fused_computation.50 | loop fusion | bytes 16777216
  25.4 7.9 %constant_dynamic-update-slice_fusion = bf16[4096,2048]{1,0:T(8,128)(2,1)} fusion(bf16[4096,2048]{1,0:T(8,128)(2,1)} %constant_dynamic-update-slice_fusion.1, bf16[4096,1024]{1,0:T(8,128)(2,1)} %param.10), kind=kLoop, calls=%fused_computation.49 | loop fusion | bytes 16777216 | tf_op jit(solution)/shard_map/concatenate | solution.py:68
  33.3 36.4 %all-gather.2.cloned.1.call-done = bf16[512,4096]{1,0:T(8,128)(2,1)} async-done(((bf16[128,4096]{1,0:T(8,128)(2,1)}), bf16[512,4096]{1,0:T(8,128)(2,1)}) %all-gather.2.cloned.1.call-update) | async-done | bytes 4194320 | tf_op jit(solution)/shard_map/all_gather | solution.py:78
  69.7 13.6 %convolution_convert_fusion.2 = bf16[512,2048]{1,0:T(8,128)(2,1)S(1)} fusion(bf16[512,4096]{1,0:T(8,128)(2,1)} %all-gather.2.cloned.1.call-done, bf16[4096,2048]{1,0:T(8,128)(2,1)} %constant_dynamic-update-slice_fusion), kind=kOutput, calls=%fused_computation.17 | convolution fusion | flops 8590983168 | bytes 23068672 | tf_op jit(solution)/shard_map/dot_general | solution.py:79
  83.3 0.2 fusion.45
  83.5 1.3 copy.31
  84.9 2.7 fusion.28
  87.6 4.9 fusion.46
  92.4 4.0 convolution_convert_fusion.3
  96.5 8.7 %fusion.24 = bf16[4,512,256]{1,2,0:T(8,128)(2,1)} fusion(bf16[512,4,256]{0,2,1:T(8,128)(2,1)S(1)} %bitcast.88, f32[4,512,512]{2,1,0:T(8,128)} %fusion.28, f32[4,512,512]{1,2,0:T(8,128)} %get-tuple-element.15, f32[4,512]{1,0:T(4,128)S(1)} %get-tuple-element.14), kind=kOutput, calls=%fused_computation.36 | convolution fusion | flops 544737792 | bytes 10493952 | tf_op jit(solution)/shard_map/hts,thd->shd/dot_general | solution.py:54
  105.2 14.1 %convolution_convert_fusion.1 = bf16[512,4096]{1,0:T(8,128)(2,1)} fusion(bf16[4096,2048]{1,0:T(8,128)(2,1)} %constant_dynamic-update-slice_fusion, bf16[512,1024]{0,1:T(8,128)(2,1)S(1)} %bitcast.91, bf16[512,1024]{0,1:T(8,128)(2,1)} %bitcast.93), kind=kOutput, calls=%fused_computation.3 | convolution fusion | flops 8596226048 | bytes 23068672 | tf_op jit(solution)/shard_map/dot_general | solution.py:98
  119.4 1.1 copy-done.9
  120.5 15.5 %convolution_convert_fusion = bf16[4096,2048]{1,0:T(8,128)(2,1)} fusion(bf16[512,4096]{1,0:T(8,128)(2,1)} %all-gather.2.cloned.1.call-done, bf16[512,1024]{0,1:T(8,128)(2,1)S(1)} %bitcast.92, bf16[512,1024]{0,1:T(8,128)(2,1)S(1)} %bitcast.94), kind=kOutput, calls=%fused_computation.2 | convolution fusion | flops 8602517504 | bytes 23068672 | tf_op jit(solution)/shard_map/dot_general | solution.py:106
  136.1 36.1 %reduce-scatter.3.cloned.1.call-done = bf16[128,4096]{1,0:T(8,128)(2,1)} async-done(((bf16[512,4096]{1,0:T(8,128)(2,1)}), bf16[128,4096]{1,0:T(8,128)(2,1)}) %reduce-scatter.3.cloned.1.call-update) | async-done | bytes 1048592 | tf_op jit(solution)/shard_map/reduce_scatter | solution.py:97
  172.2 2.9 convolution_convert_fusion.4
  175.1 1.3 copy.25
  176.5 9.0 %fusion.25 = bf16[4,256,512]{2,1,0:T(8,128)(2,1)S(1)} fusion(bf16[512,4,256]{0,2,1:T(8,128)(2,1)} %bitcast.85, f32[4,512,512]{2,1,0:T(8,128)} %fusion.28, f32[4,512,512]{1,2,0:T(8,128)} %get-tuple-element.15, f32[4,512]{1,0:T(4,128)S(1)} %get-tuple-element.14), kind=kOutput, calls=%fused_computation.37 | convolution fusion | flops 544737792 | bytes 10493952 | tf_op jit(solution)/shard_map/hts,shd->thd/dot_general | solution.py:51
  185.5 1.3 copy.26
  186.8 0.4 fusion.17
  187.2 1.7 fusion.26
  188.9 310.9 %reduce-scatter.5.cloned.1.call-done = bf16[512,2048]{1,0:T(8,128)(2,1)} async-done(((bf16[4096,2048]{1,0:T(8,128)(2,1)}), bf16[512,2048]{1,0:T(8,128)(2,1)}) %reduce-scatter.5.cloned.1.call-update) | async-done | bytes 2097168 | tf_op jit(solution)/shard_map/reduce_scatter | solution.py:109
  499.8 4.0 fusion.44
  (27 shorter events, 0.2 us)
Async XLA Ops:
  7.2 7.2 %copy-start.1 = (bf16[1,512,1024]{2,1,0:T(8,128)(2,1)S(1)}, bf16[1,512,1024]{2,1,0:T(8,128)(2,1)}, u32[]{:S(2)}) copy-start(bf16[1,512,1024]{2,1,0:T(8,128)(2,1)} %param.11) | copy-start | bytes 3145732
  7.2 8.5 %copy-start.2 = (bf16[1,512,1024]{2,1,0:T(8,128)(2,1)S(1)}, bf16[1,512,1024]{2,1,0:T(8,128)(2,1)}, u32[]{:S(2)}) copy-start(bf16[1,512,1024]{2,1,0:T(8,128)(2,1)} %param.12) | copy-start | bytes 3145732
  7.2 9.0 %copy-start.7 = (s32[8]{0:T(128)S(1)}, s32[8]{0:T(128)}, u32[]{:S(2)}) copy-start(s32[8]{0:T(128)} %param.13) | copy-start | bytes 100
  7.2 62.5 %all-gather.2.cloned.1.call-start = ((), (), s32[]{:S(2)}) async-start(), calls=%async_computation.2 | async-start | bytes 5242880 | tf_op jit(solution)/shard_map/all_gather | solution.py:78
  10.5 2.8 collective-permute-start
  13.3 1.0 copy-start.3
  14.3 157.9 %reduce-scatter.3.cloned.1.call-start = ((), (), s32[]{:S(2)}) async-start(), calls=%async_computation.3 | async-start | bytes 5242880 | tf_op jit(solution)/shard_map/reduce_scatter | solution.py:97
  84.9 2.7 copy-start.4
  92.4 4.0 copy-start.5
  96.5 8.7 %copy-start.8 = (bf16[4,512,256]{1,2,0:T(8,128)(2,1)S(1)}, bf16[4,512,256]{1,2,0:T(8,128)(2,1)}, u32[]{:S(2)}) copy-start(bf16[4,512,256]{1,2,0:T(8,128)(2,1)} %convolution_convert_fusion.3) | copy-start | bytes 3145732
  119.3 1.2 copy-start.9
  119.3 380.5 %reduce-scatter.5.cloned.1.call-start = ((), (), s32[]{:S(2)}) async-start(), calls=%async_computation.4 | async-start | bytes 18874368 | tf_op jit(solution)/shard_map/reduce_scatter | solution.py:109
  172.2 14.6 %collective-permute-start.1 = (bf16[128,4096]{1,0:T(8,128)(2,1)}, bf16[128,4096]{1,0:T(8,128)(2,1)S(1)}, u32[]{:S(2)}, u32[]{:S(2)}) collective-permute-start(bf16[128,4096]{1,0:T(8,128)(2,1)} %reduce-scatter.3.cloned.1.call-done), channel_id=1, source_target_pairs={{0,16},{16,0},{1,17},{17,1},{2,18},{18,2},{3,19},{19,3},{4,20},{20... | collective-permute-start | bytes 3145736 | tf_op jit(solution)/shard_map/ppermute | solution.py:16
  176.5 10.3 %copy-start = (bf16[1,128,4096]{2,1,0:T(8,128)(2,1)S(1)}, bf16[1,128,4096]{2,1,0:T(8,128)(2,1)}, u32[]{:S(2)}) copy-start(bf16[1,128,4096]{2,1,0:T(8,128)(2,1)} %param.7) | copy-start | bytes 3145732
  176.5 10.3 %copy-start.6 = (f32[4096]{0:T(1024)S(1)}, f32[4096]{0:T(1024)}, u32[]{:S(2)}) copy-start(f32[4096]{0:T(1024)} %param.8) | copy-start | bytes 49156
Sparse Core Ops, SparseCore 0:
  14.4 55.3 all-gather.1
  119.5 52.6 reduce-scatter.2
  174.7 325.1 reduce-scatter.4
where the time goes:
time: 511 us; the launch traced here: 510 us
  waiting for transfers between devices  386 us (76%)
  matrix products  75.5 us (15%)
  local copies, waits for them, and re-layouts  28.6 us (6%)
  between operations  13.9 us (3%)
  other arithmetic  5.99 us (1%)
    reduce_scatter x1, waiting for transfers between devices, on_device(): lax.psum_scatter(weight_term.astype(jnp.bfloat16), ('section', 'dp'), sca...  311 us
    all_gather x1, waiting for transfers between devices, on_device(): gathered = lax.all_gather(partner_rows, 'seq', axis=0, tiled=True)  36.4 us
    reduce_scatter x1, waiting for transfers between devices, on_device(): lax.psum_scatter(lax.dot_general(kv_grads, projection, (((1,), (1,)), (()...  36.1 us
    dot_general x1, matrix products, on_device(): lax.dot_general(gathered, kv_grads, (((0,), (0,)), ((), ())), preferred_e...  15.5 us
    dot_general x1, matrix products, on_device(): lax.dot_general(kv_grads, projection, (((1,), (1,)), ((), ())), preferred...  14.1 us
    dot_general x1, matrix products, on_device(): jnp.dot(gathered, projection, preferred_element_type=jnp.float32)  13.6 us
    unnamed x23, local copies, waits for them, and re-layouts  12.7 us
  transfers between devices with their start and end apart: 5, of which 4 were waited for; matrix products, arithmetic and copies ran while one was open for 10% of the time, Pallas kernels for 0%

commit v1 on v0

v1 whole, which is shorter than its diff:
```python
import jax
import jax.numpy as jnp
from jax import lax
from jax.experimental import pallas as pl
from jax.experimental.pallas import tpu as pltpu
from jax.sharding import PartitionSpec as P

HD = 256


EPS = 1e-06
NEG_FILL = -1e30
BF16 = jnp.bfloat16
F32 = jnp.float32


def swap(value, axis, mask):
    pairs = [(source, source ^ mask) for source in range(lax.axis_size(axis))]
    return lax.ppermute(value, axis, pairs)


def normalize(enc_rows, gain):
    wide_rows = enc_rows.astype(F32)
    factor = lax.rsqrt(jnp.mean(wide_rows * wide_rows, axis=-1, keepdims=True) + EPS)
    return ((wide_rows * factor * gain).astype(BF16), factor)


def norm_backward(enc_rows, factor, gain, row_grad):
    wide_rows = enc_rows.astype(F32)
    scaled = row_grad.astype(F32) * gain
    inner_sum = jnp.mean(scaled * wide_rows, axis=-1, keepdims=True)
    return (factor * scaled - wide_rows * factor * factor * factor * inner_sum).astype(BF16)


def gather_blocks(own):
    count = lax.axis_size("seq")
    if count == 4:
        half = own.shape[0] // 2
        top, bottom = own[:half], own[half:]
        first_top, second_bottom = swap(top, "seq", 1), swap(bottom, "seq", 2)
        first_bottom, second_top = swap(bottom, "seq", 1), swap(top, "seq", 2)
        third_top, third_bottom = swap(first_top, "seq", 2), swap(second_bottom, "seq", 1)
        return [
            own,
            jnp.concatenate([first_top, first_bottom]),
            jnp.concatenate([second_top, second_bottom]),
            jnp.concatenate([third_top, third_bottom]),
        ]
    blocks = [own]
    bit = 1
    while bit < count:
        blocks = blocks + [swap(block, "seq", bit) for block in blocks]
        bit *= 2
    return blocks


def dot(left, right, left_dim, right_dim):
    return lax.dot_general(
        left, right, (((left_dim,), (right_dim,)), ((), ())), preferred_element_type=F32
    )


def attend_kernel(
    visible, query, key_early, key_late, value_early, value_late, upstream, attended, query_grad, kv_grad
):
    score_scale = HD ** (-0.5)
    query_rows, upstream_rows = query[...], upstream[...]
    key_rows = jnp.concatenate([key_early[...], key_late[...]], axis=0)
    value_rows = jnp.concatenate([value_early[...], value_late[...]], axis=0)
    scores = dot(key_rows, query_rows, 1, 1) * score_scale
    scores = jnp.where(visible[...] > 0, scores, NEG_FILL)
    exponent = jnp.exp(scores - jnp.max(scores, axis=0, keepdims=True))
    probability = exponent * (1.0 / jnp.sum(exponent, axis=0, keepdims=True))
    prob_weights = probability.astype(BF16)
    grad_probs = dot(value_rows, upstream_rows, 1, 1)
    inner_sum = jnp.sum(probability * grad_probs, axis=0, keepdims=True)
    grad_scores = (probability * (grad_probs - inner_sum) * score_scale).astype(BF16)
    kv_grad[:, :HD] = dot(grad_scores, query_rows, 1, 0).astype(BF16)
    kv_grad[:, HD:] = dot(prob_weights, upstream_rows, 1, 0).astype(BF16)
    attended[...] = dot(prob_weights, value_rows, 0, 0).astype(BF16)
    query_grad[...] = dot(grad_scores, key_rows, 0, 0).astype(BF16)


def attend_head(head, visible, query, key_early, key_late, value_early, value_late, upstream):
    src_rows, target_rows = visible.shape[0], query.shape[0]

    def column(rows):
        return pl.BlockSpec((rows, HD), lambda step: (0, head))

    def whole(rows, columns):
        return pl.BlockSpec((rows, columns), lambda step: (0, 0))

    early, late = key_early.shape[0], key_late.shape[0]
    return pl.pallas_call(
        attend_kernel,
        grid=(1,),
        in_specs=[
            whole(src_rows, 1),
            column(target_rows),
            column(early),
            column(late),
            column(early),
            column(late),
            column(target_rows),
        ],
        out_specs=[
            whole(target_rows, HD),
            whole(target_rows, HD),
            whole(src_rows, 2 * HD),
        ],
        out_shape=[
            jax.ShapeDtypeStruct((target_rows, HD), BF16),
            jax.ShapeDtypeStruct((target_rows, HD), BF16),
            jax.ShapeDtypeStruct((src_rows, 2 * HD), BF16),
        ],
        compiler_params=pltpu.CompilerParams(vmem_limit_bytes=48 * 1024 * 1024),
        cost_estimate=pl.CostEstimate(
            flops=12 * src_rows * target_rows * HD,
            bytes_accessed=2 * HD * (4 * target_rows + 4 * src_rows),
            transcendentals=src_rows * target_rows,
        ),
    )(visible, query, key_early, key_late, value_early, value_late, upstream)


def on_device(enc_states, enc_gain, key_weight, value_weight, queries, out_grad, lengths):
    enc_rows = enc_states[0]
    own_rows, width = enc_rows.shape
    heads_here = key_weight.shape[1] // HD
    section_count, dp_count, seq_count = (lax.axis_size(name) for name in ("section", "dp", "seq"))
    section, place, seq = (lax.axis_index(name) for name in ("section", "dp", "seq"))
    partner = (section * dp_count + place + dp_count) % (section_count * dp_count)
    src_rows = own_rows * seq_count
    section_width = width // section_count
    target_width = section_width // dp_count

    normed, factor = normalize(enc_rows, enc_gain)
    partner_rows = swap(normed, "section", 1)
    blocks = gather_blocks(partner_rows)
    quarter = seq_count // 4
    quarters = [
        blocks[step] if quarter == 1 else jnp.concatenate(blocks[step * quarter : (step + 1) * quarter])
        for step in range(4)
    ]
    block_start = (seq ^ jnp.arange(seq_count, dtype=jnp.int32)) * own_rows
    positions = block_start[:, None] + jnp.arange(own_rows, dtype=jnp.int32)[None, :]
    visible = (positions.reshape(src_rows, 1) < lengths[partner]).astype(jnp.int32)

    early, late = jnp.concatenate(quarters[:3]), quarters[3]
    key_early, value_early, key_late, value_late = (
        jnp.dot(rows, weight, preferred_element_type=F32).astype(BF16)
        for rows, weight in ((early, key_weight), (early, value_weight), (late, key_weight), (late, value_weight))
    )

    inward = [(0, 1), (3, 2)]
    outward = [(1, 0), (2, 3)]
    across = [(1, 2), (2, 1)]

    def features(rows, xor):
        start = (place ^ xor) * target_width
        return lax.dynamic_slice_in_dim(rows, start, target_width, axis=1)

    mine, theirs, far_mine, far_theirs = [], [], [], []
    for rows in quarters:
        here = lax.dynamic_slice_in_dim(rows, section * section_width, section_width, axis=1)
        away = lax.dynamic_slice_in_dim(rows, (1 - section) * section_width, section_width, axis=1)
        there = swap(away, "section", 1)
        mine.append(here)
        theirs.append(there)
        far = [
            jnp.concatenate([features(half, 3), features(half, 2)], axis=1) for half in (here, there)
        ]
        far = lax.ppermute(jnp.concatenate(far), "dp", inward)
        far_mine.append(far[: far.shape[0] // 2])
        far_theirs.append(far[far.shape[0] // 2 :])
    chip_rows = jnp.concatenate(mine + theirs)
    chip_features = [features(chip_rows, xor) for xor in range(4)]
    outer_far = jnp.concatenate(far_mine + far_theirs)
    outer_features = {2: outer_far[:, :target_width], 3: outer_far[:, target_width:]}
    outer_features[0] = lax.ppermute(chip_features[1], "dp", inward)

    attended, query_grad, kv_grads, sums = [], [], [], []
    for head in range(heads_here):
        head_attended, head_query_grad, kv_grad = attend_head(
            head, visible, queries[0], key_early, key_late, value_early, value_late, out_grad[0]
        )
        attended.append(head_attended)
        query_grad.append(head_query_grad)
        kv_grads.append(kv_grad)
        chip_grad = jnp.concatenate([kv_grad, swap(kv_grad, "section", 1)])
        outer_grad = lax.ppermute(kv_grad, "dp", inward)
        outer_grad = jnp.concatenate([outer_grad, swap(outer_grad, "section", 1)])

        def pair_sum(xor):
            return dot(chip_features[xor], chip_grad, 0, 0) + dot(outer_features[xor], outer_grad, 0, 0)

        to_outer = lax.ppermute(pair_sum(2).astype(BF16), "dp", across)
        to_inner = lax.ppermute(pair_sum(3).astype(BF16), "dp", across)
        relay = (dot(chip_features[1], chip_grad, 0, 0) + to_outer.astype(F32)).astype(BF16)
        relay = lax.ppermute(relay, "dp", outward)
        sums.append(pair_sum(0) + to_inner.astype(F32) + relay.astype(F32))

    key_rows_grad = jnp.concatenate([kv_grad[:, :HD] for kv_grad in kv_grads], axis=1)
    value_rows_grad = jnp.concatenate([kv_grad[:, HD:] for kv_grad in kv_grads], axis=1)
    row_term = (dot(key_rows_grad, key_weight, 1, 1) + dot(value_rows_grad, value_weight, 1, 1)).astype(BF16)
    row_share = row_term[:own_rows].astype(F32)
    for step in range(1, seq_count):
        row_share = row_share + swap(
            row_term[step * own_rows : (step + 1) * own_rows], "seq", step
        ).astype(F32)
    row_grad = swap(row_share.astype(BF16), "section", 1)
    enc_grad = norm_backward(enc_rows, factor, enc_gain, row_grad)
    return (
        jnp.concatenate(attended, axis=1)[None],
        enc_grad[None],
        jnp.concatenate([total[:, :HD] for total in sums], axis=1),
        jnp.concatenate([total[:, HD:] for total in sums], axis=1),
        jnp.concatenate(query_grad, axis=1)[None],
    )


def solution(mesh):
    placed = (
        P(("section", "dp"), "seq", None),
        P(),
        P(None, "seq"),
        P(None, "seq"),
        P(("section", "dp"), None, "seq"),
        P(("section", "dp"), None, "seq"),
        P(),
    )
    return jax.shard_map(
        on_device,
        mesh=mesh,
        in_specs=placed,
        out_specs=(
            P(("section", "dp"), None, "seq"),
            P(("section", "dp"), "seq", None),
            P(("section", "dp"), "seq"),
            P(("section", "dp"), "seq"),
            P(("section", "dp"), None, "seq"),
        ),
        check_vma=False,
    )
```

time: 511 us -> 343 us (0.67); the launches traced: 510 us -> 337 us
  waiting for transfers between devices: 386 us -> 170 us
  starting transfers between devices: 0.64 us -> 62.8 us
  matrix products: 75.5 us -> 53.7 us
  between operations: 13.9 us -> 1.99 us
  other arithmetic: 5.99 us -> 15.8 us
  Pallas kernels: 0 us -> 5.84 us
    reduce_scatter x2 -> x0, waiting for transfers between devices: 347 us -> none  [the longest x1 311 us: on_device(): lax.psum_scatter(weight_term.astype(jnp.bfloat16), ('section', 'dp'), sca...]
    ppermute x2 -> x44, waiting for transfers between devices: 2.29 us -> 170 us  [the longest x4 86.1 us: on_device(): relay = lax.ppermute(relay, 'dp', outward)]
    ppermute x2 -> x44, starting transfers between devices: 0.52 us -> 62.8 us  [the longest x4 25.6 us: on_device(): far = lax.ppermute(jnp.concatenate(far), 'dp', inward)]
    all_gather x1 -> x0, waiting for transfers between devices: 36.4 us -> none  [on_device(): gathered = lax.all_gather(partner_rows, 'seq', axis=0, tiled=True)]
    dot_general x8 -> x34, matrix products: 70.6 us -> 53.7 us  [the longest x30 44.4 us: dot(): lax.dot_general(left, right, (((left_dim,), (right_dim,)), ((), ())), pre...]
    concatenate x1 -> x13, local copies, waits for them, and re-layouts: 7.93 us -> 1.62 us  [the longest x4 1.18 us: on_device(): chip_grad = jnp.concatenate([kv_grad, swap(kv_grad, 'section', 1)])]
    pallas_call x0 -> x4, Pallas kernels: none -> 5.84 us  [attend_head(): pl.pallas_call(attend_kernel, grid=(1,), in_specs=[whole(src_rows, 1), co...]
    unnamed x23 -> x62, local copies, waits for them, and re-layouts: 12.7 us -> 11.2 us
  transfers between devices with their start and end apart: 5 -> 44, of which waited for: 4 -> 14; matrix products, arithmetic and copies ran while one was open for 10% -> 25% of each run, Pallas kernels for 0% -> 2%
where the time goes in v1:
time: 343 us; the launch traced here: 337 us
  waiting for transfers between devices  170 us (50%)
  starting transfers between devices  62.8 us (18%)
  matrix products  53.7 us (16%)
  local copies, waits for them, and re-layouts  26.4 us (8%)
  other arithmetic  15.8 us (5%)
  Pallas kernels  5.84 us (2%)
    ppermute x4, waiting for transfers between devices, on_device(): relay = lax.ppermute(relay, 'dp', outward)  86.1 us
    ppermute x23, waiting for transfers between devices, swap(): return lax.ppermute(value, axis, pairs)  49.8 us
    dot_general x30, matrix products, dot(): lax.dot_general(left, right, (((left_dim,), (right_dim,)), ((), ())), pre...  44.4 us
    ppermute x4, starting transfers between devices, on_device(): far = lax.ppermute(jnp.concatenate(far), 'dp', inward)  25.6 us
    ppermute x4, waiting for transfers between devices, on_device(): far = lax.ppermute(jnp.concatenate(far), 'dp', inward)  17.8 us
    ppermute x4, waiting for transfers between devices, on_device(): outer_grad = lax.ppermute(kv_grad, 'dp', inward)  16.3 us
    ppermute x23, starting transfers between devices, swap(): return lax.ppermute(value, axis, pairs)  15 us
    unnamed x62, local copies, waits for them, and re-layouts  11.2 us
  transfers between devices with their start and end apart: 44, of which 14 were waited for; matrix products, arithmetic and copies ran while one was open for 25% of the time, Pallas kernels for 2%

profile of v1, /device:TPU:0, one launch (start us, length us, event | category | flops | bytes accessed | tf_op | source)
XLA Modules:
  0.0 336.5 jit_solution(5892187208178048511)
XLA Ops:
  6.6 2.9 collective-permute-start.1
  12.1 10.2 %collective-permute-done.1 = bf16[64,4096]{1,0:T(8,128)(2,1)S(1)} collective-permute-done((bf16[64,4096]{1,0:T(8,128)(2,1)S(1)}, bf16[64,4096]{1,0:T(8,128)(2,1)S(1)}, u32[]{:S(2)}, u32[]{:S(2)}) %collective-permute-start.1) | collective-permute-done | bytes 524320 | tf_op jit(solution)/shard_map/ppermute | solution.py:19
  22.4 10.6 %collective-permute-done.2 = bf16[64,4096]{1,0:T(8,128)(2,1)S(1)} collective-permute-done((bf16[64,4096]{1,0:T(8,128)(2,1)S(1)}, bf16[64,4096]{1,0:T(8,128)(2,1)S(1)}, u32[]{:S(2)}, u32[]{:S(2)}) %collective-permute-start.2) | collective-permute-done | bytes 524320 | tf_op jit(solution)/shard_map/ppermute | solution.py:19
  35.7 1.9 copy-done.5
  37.6 3.4 %convolution_convert_fusion.value_early = bf16[384,1024]{1,0:T(8,128)(2,1)S(1)} fusion(bf16[384,4096]{1,0:T(8,128)(2,1)S(1)} %get-tuple-element.77, bf16[4096,1024]{1,0:T(8,128)(2,1)S(1)} %bitcast.73), kind=kOutput, calls=%fused_computation.17 | convolution fusion | flops 3221618688 | bytes 12320768 | tf_op jit(solution)/shard_map/dot_general | solution.py:150
  42.6 3.4 %convolution_convert_fusion.1.key_early = bf16[384,1024]{1,0:T(8,128)(2,1)S(1)} fusion(bf16[384,4096]{1,0:T(8,128)(2,1)S(1)} %get-tuple-element.77, bf16[4096,1024]{1,0:T(8,128)(2,1)S(1)} %bitcast.71), kind=kOutput, calls=%fused_computation.18 | convolution fusion | flops 3221618688 | bytes 12320768 | tf_op jit(solution)/shard_map/dot_general | solution.py:150
  47.0 15.5 %collective-permute-start.19 = (bf16[256,1024]{1,0:T(8,128)(2,1)}, bf16[256,1024]{1,0:T(8,128)(2,1)}, u32[]{:S(2)}, u32[]{:S(2)}) collective-permute-start(bf16[256,1024]{1,0:T(8,128)(2,1)} %maximum_maximum_fusion), channel_id=1, source_target_pairs={{0,4},{12,8},{1,5},{13,9},{2,6},{14,10},{3,7},{15,11},{16,20},{28,... | collective-permute-start | bytes 1572872 | tf_op jit(solution)/shard_map/ppermute | solution.py:172
  65.8 10.5 %collective-permute-done.6 = bf16[64,4096]{1,0:T(8,128)(2,1)S(1)} collective-permute-done((bf16[64,4096]{1,0:T(8,128)(2,1)S(1)}, bf16[64,4096]{1,0:T(8,128)(2,1)S(1)}, u32[]{:S(2)}, u32[]{:S(2)}) %collective-permute-start.6) | collective-permute-done | bytes 524320 | tf_op jit(solution)/shard_map/ppermute | solution.py:19
  81.2 2.1 collective-permute-start.17
  90.8 10.2 %fusion.30 = f32[512,4096]{1,0:T(8,128)} fusion(bf16[4096,1024]{1,0:T(8,128)(2,1)} %param.9, bf16[512,256]{1,0:T(8,128)(2,1)S(1)} %get-tuple-element.91, bf16[512,256]{1,0:T(8,128)(2,1)S(1)} %get-tuple-element.89, bf16[512,256]{1,0:T(8,128)(2,1)S(1)} %get-tuple-element.87, bf16[512,256]{1,0:T(8,128)(2,1)S(1)} %get-tuple-element.85), kind=kOutput, calls=%fused_computation.59 | convolution fusion | flops 4299161600 | bytes 17825792 | tf_op jit(solution)/shard_map/dot_general | solution.py:58
  101.0 12.7 %add_convert_fusion = bf16[512,4096]{1,0:T(8,128)(2,1)} fusion(f32[512,4096]{1,0:T(8,128)} %fusion.30, bf16[4096,1024]{1,0:T(8,128)(2,1)} %param.10, bf16[512,256]{1,0:T(8,128)(2,1)} %get-tuple-element.90, bf16[512,256]{1,0:T(8,128)(2,1)} %get-tuple-element.88, bf16[512,256]{1,0:T(8,128)(2,1)} %get-tuple-element.86, bf16[512,256]{1,0:T(8,128)(2,1)S(1)} %get-tuple-element.84), kind=kOutput, calls=%fused_computation | convolution fusion | flops 4303355904 | bytes 22020096 | tf_op jit(solution)/shard_map/dot_general | solution.py:58
  113.7 2.2 fusion.88
  118.0 1.6 maximum_bitcast_fusion
  123.0 1.7 collective-permute-start.33
  127.8 5.7 %collective-permute-done.27 = bf16[512,512]{1,0:T(8,128)(2,1)S(1)} collective-permute-done((bf16[512,512]{1,0:T(8,128)(2,1)S(1)}, bf16[512,512]{1,0:T(8,128)(2,1)S(1)}, u32[]{:S(2)}, u32[]{:S(2)}) %collective-permute-start.27) | collective-permute-done | bytes 524320 | tf_op jit(solution)/shard_map/ppermute | solution.py:190
  133.5 4.4 %collective-permute-start.39 = (bf16[512,512]{1,0:T(8,128)(2,1)S(1)}, bf16[512,512]{1,0:T(8,128)(2,1)S(1)}, u32[]{:S(2)}, u32[]{:S(2)}) collective-permute-start(bf16[512,512]{1,0:T(8,128)(2,1)S(1)} %get-tuple-element.24), channel_id=1, source_target_pairs={{0,4},{12,8},{1,5},{13,9},{2,6},{14,10},{3,7},{15,11},{16,20},{28,... | collective-permute-start | bytes 1572872 | tf_op jit(solution)/shard_map/ppermute | solution.py:190
  138.7 6.0 %collective-permute-done.33 = bf16[512,512]{1,0:T(8,128)(2,1)S(1)} collective-permute-done((bf16[512,512]{1,0:T(8,128)(2,1)S(1)}, bf16[512,512]{1,0:T(8,128)(2,1)S(1)}, u32[]{:S(2)}, u32[]{:S(2)}) %collective-permute-start.33) | collective-permute-done | bytes 524320 | tf_op jit(solution)/shard_map/ppermute | solution.py:190
  144.7 4.4 %collective-permute-start.21 = (bf16[256,1024]{1,0:T(8,128)(2,1)S(1)}, bf16[256,1024]{1,0:T(8,128)(2,1)S(1)}, u32[]{:S(2)}, u32[]{:S(2)}) collective-permute-start(bf16[256,1024]{1,0:T(8,128)(2,1)S(1)} %maximum_maximum_fusion.2), channel_id=1, source_target_pairs={{0,4},{12,8},{1,5},{13,9},{2,6},{14,10},{3,7},{15,11},{16,20},{28,... | collective-permute-start | bytes 1572872 | tf_op jit(solution)/shard_map/ppermute | solution.py:172
  151.3 4.6 %collective-permute-done.39 = bf16[512,512]{1,0:T(8,128)(2,1)S(1)} collective-permute-done((bf16[512,512]{1,0:T(8,128)(2,1)S(1)}, bf16[512,512]{1,0:T(8,128)(2,1)S(1)}, u32[]{:S(2)}, u32[]{:S(2)}) %collective-permute-start.39) | collective-permute-done | bytes 524320 | tf_op jit(solution)/shard_map/ppermute | solution.py:190
  160.5 17.7 %collective-permute-done.20 = bf16[256,1024]{1,0:T(8,128)(2,1)S(1)} collective-permute-done((bf16[256,1024]{1,0:T(8,128)(2,1)S(1)}, bf16[256,1024]{1,0:T(8,128)(2,1)S(1)}, u32[]{:S(2)}, u32[]{:S(2)}) %collective-permute-start.20) | collective-permute-done | bytes 524320 | tf_op jit(solution)/shard_map/ppermute | solution.py:172
  178.2 4.4 %collective-permute-start.22 = (bf16[256,1024]{1,0:T(8,128)(2,1)S(1)}, bf16[256,1024]{1,0:T(8,128)(2,1)S(1)}, u32[]{:S(2)}, u32[]{:S(2)}) collective-permute-start(bf16[256,1024]{1,0:T(8,128)(2,1)S(1)} %maximum_maximum_fusion.3), channel_id=1, source_target_pairs={{0,4},{12,8},{1,5},{13,9},{2,6},{14,10},{3,7},{15,11},{16,20},{28,... | collective-permute-start | bytes 1572872 | tf_op jit(solution)/shard_map/ppermute | solution.py:172
  187.2 17.3 %collective-permute-done.8 = bf16[128,4096]{1,0:T(8,128)(2,1)S(1)} collective-permute-done((bf16[128,4096]{1,0:T(8,128)(2,1)S(1)}, bf16[128,4096]{1,0:T(8,128)(2,1)S(1)}, u32[]{:S(2)}, u32[]{:S(2)}) %collective-permute-start.8) | collective-permute-done | bytes 1048608 | tf_op jit(solution)/shard_map/ppermute | solution.py:19
  205.0 2.9 add_convert_fusion.1
  229.7 57.1 %collective-permute-done.25 = bf16[512,512]{0,1:T(8,128)(2,1)S(1)} collective-permute-done((bf16[512,512]{0,1:T(8,128)(2,1)S(1)}, bf16[512,512]{0,1:T(8,128)(2,1)S(1)}, u32[]{:S(2)}, u32[]{:S(2)}) %collective-permute-start.25) | collective-permute-done | bytes 524320 | tf_op jit(solution)/shard_map/ppermute | solution.py:199
  290.5 13.4 %collective-permute-done.31 = bf16[512,512]{0,1:T(8,128)(2,1)S(1)} collective-permute-done((bf16[512,512]{0,1:T(8,128)(2,1)S(1)}, bf16[512,512]{0,1:T(8,128)(2,1)S(1)}, u32[]{:S(2)}, u32[]{:S(2)}) %collective-permute-start.31) | collective-permute-done | bytes 524320 | tf_op jit(solution)/shard_map/ppermute | solution.py:199
  306.3 8.9 %collective-permute-done.37 = bf16[512,512]{0,1:T(8,128)(2,1)S(1)} collective-permute-done((bf16[512,512]{0,1:T(8,128)(2,1)S(1)}, bf16[512,512]{0,1:T(8,128)(2,1)S(1)}, u32[]{:S(2)}, u32[]{:S(2)}) %collective-permute-start.37) | collective-permute-done | bytes 524320 | tf_op jit(solution)/shard_map/ppermute | solution.py:199
  317.7 6.8 %collective-permute-done.43 = bf16[512,512]{0,1:T(8,128)(2,1)S(1)} collective-permute-done((bf16[512,512]{0,1:T(8,128)(2,1)S(1)}, bf16[512,512]{0,1:T(8,128)(2,1)S(1)}, u32[]{:S(2)}, u32[]{:S(2)}) %collective-permute-start.43) | collective-permute-done | bytes 524320 | tf_op jit(solution)/shard_map/ppermute | solution.py:199
  326.4 1.8 copy.59
  328.2 1.7 pad_maximum_fusion
  329.9 1.8 copy.58
  331.7 1.6 fusion.8
  333.4 2.9 fusion.29
  (211 shorter events, 82.1 us)
Async XLA Ops:
  9.5 24.5 %collective-permute-start.3 = (bf16[64,4096]{1,0:T(8,128)(2,1)S(1)}, bf16[64,4096]{1,0:T(8,128)(2,1)S(1)}, u32[]{:S(2)}, u32[]{:S(2)}) collective-permute-start(bf16[64,4096]{1,0:T(8,128)(2,1)S(1)} %get-tuple-element.67), channel_id=1, source_target_pairs={{0,2},{1,3},{2,0},{3,1},{4,6},{5,7},{6,4},{7,5},{8,10},{9,11},{10,... | collective-permute-start | bytes 1572872 | tf_op jit(solution)/shard_map/ppermute | solution.py:19
  11.1 21.9 %collective-permute-start.2 = (bf16[64,4096]{1,0:T(8,128)(2,1)S(1)}, bf16[64,4096]{1,0:T(8,128)(2,1)S(1)}, u32[]{:S(2)}, u32[]{:S(2)}) collective-permute-start(bf16[64,4096]{1,0:T(8,128)(2,1)S(1)} %get-tuple-element.66), channel_id=1, source_target_pairs={{0,1},{1,0},{2,3},{3,2},{4,5},{5,4},{6,7},{7,6},{8,9},{9,8},{10,11... | collective-permute-start | bytes 1572872 | tf_op jit(solution)/shard_map/ppermute | solution.py:19
  11.6 22.9 %collective-permute-start.4 = (bf16[64,4096]{1,0:T(8,128)(2,1)S(1)}, bf16[64,4096]{1,0:T(8,128)(2,1)S(1)}, u32[]{:S(2)}, u32[]{:S(2)}) collective-permute-start(bf16[64,4096]{1,0:T(8,128)(2,1)S(1)} %get-tuple-element.66), channel_id=1, source_target_pairs={{0,2},{1,3},{2,0},{3,1},{4,6},{5,7},{6,4},{7,5},{8,10},{9,11},{10,... | collective-permute-start | bytes 1572872 | tf_op jit(solution)/shard_map/ppermute | solution.py:19
  11.7 34.3 %collective-permute-start.11 = (bf16[128,2048]{1,0:T(8,128)(2,1)S(1)}, bf16[128,2048]{1,0:T(8,128)(2,1)S(1)}, u32[]{:S(2)}, u32[]{:S(2)}) collective-permute-start(bf16[128,2048]{1,0:T(8,128)(2,1)S(1)} %get-tuple-element.64), channel_id=1, source_target_pairs={{0,16},{16,0},{1,17},{17,1},{2,18},{18,2},{3,19},{19,3},{4,20},{20... | collective-permute-start | bytes 1572872 | tf_op jit(solution)/shard_map/ppermute | solution.py:19
  34.0 82.9 %collective-permute-start.12 = (bf16[128,2048]{1,0:T(8,128)(2,1)}, bf16[128,2048]{1,0:T(8,128)(2,1)S(1)}, u32[]{:S(2)}, u32[]{:S(2)}) collective-permute-start(bf16[128,2048]{1,0:T(8,128)(2,1)} %get-tuple-element.62), channel_id=1, source_target_pairs={{0,16},{16,0},{1,17},{17,1},{2,18},{18,2},{3,19},{19,3},{4,20},{20... | collective-permute-start | bytes 1572872 | tf_op jit(solution)/shard_map/ppermute | solution.py:19
  35.5 82.0 %collective-permute-start.13 = (bf16[128,2048]{1,0:T(8,128)(2,1)}, bf16[128,2048]{1,0:T(8,128)(2,1)S(1)}, u32[]{:S(2)}, u32[]{:S(2)}) collective-permute-start(bf16[128,2048]{1,0:T(8,128)(2,1)} %get-tuple-element.60), channel_id=1, source_target_pairs={{0,16},{16,0},{1,17},{17,1},{2,18},{18,2},{3,19},{19,3},{4,20},{20... | collective-permute-start | bytes 1572872 | tf_op jit(solution)/shard_map/ppermute | solution.py:19
  41.0 24.7 %collective-permute-start.5 = (bf16[64,4096]{1,0:T(8,128)(2,1)S(1)}, bf16[64,4096]{1,0:T(8,128)(2,1)S(1)}, u32[]{:S(2)}, u32[]{:S(2)}) collective-permute-start(bf16[64,4096]{1,0:T(8,128)(2,1)S(1)} %collective-permute-done.1), channel_id=1, source_target_pairs={{0,2},{1,3},{2,0},{3,1},{4,6},{5,7},{6,4},{7,5},{8,10},{9,11},{10,... | collective-permute-start | bytes 1572872 | tf_op jit(solution)/shard_map/ppermute | solution.py:19
  47.0 72.8 %collective-permute-start.19 = (bf16[256,1024]{1,0:T(8,128)(2,1)}, bf16[256,1024]{1,0:T(8,128)(2,1)}, u32[]{:S(2)}, u32[]{:S(2)}) collective-permute-start(bf16[256,1024]{1,0:T(8,128)(2,1)} %maximum_maximum_fusion), channel_id=1, source_target_pairs={{0,4},{12,8},{1,5},{13,9},{2,6},{14,10},{3,7},{15,11},{16,20},{28,... | collective-permute-start | bytes 1572872 | tf_op jit(solution)/shard_map/ppermute | solution.py:172
  81.1 41.9 %collective-permute-start.15 = (bf16[512,512]{1,0:T(8,128)(2,1)S(1)}, bf16[512,512]{1,0:T(8,128)(2,1)}, u32[]{:S(2)}, u32[]{:S(2)}) collective-permute-start(bf16[512,512]{1,0:T(8,128)(2,1)S(1)} %get-tuple-element.21), channel_id=1, source_target_pairs={{0,16},{16,0},{1,17},{17,1},{2,18},{18,2},{3,19},{19,3},{4,20},{20... | collective-permute-start | bytes 1572872 | tf_op jit(solution)/shard_map/ppermute | solution.py:19
  81.2 45.4 %collective-permute-start.17 = (bf16[512,512]{1,0:T(8,128)(2,1)S(1)}, bf16[512,512]{1,0:T(8,128)(2,1)}, u32[]{:S(2)}, u32[]{:S(2)}) collective-permute-start(bf16[512,512]{1,0:T(8,128)(2,1)S(1)} %get-tuple-element.21), channel_id=1, source_target_pairs={{0,4},{12,8},{1,5},{13,9},{2,6},{14,10},{3,7},{15,11},{16,20},{28,... | collective-permute-start | bytes 1572872 | tf_op jit(solution)/shard_map/ppermute | solution.py:190
  116.9 32.2 %collective-permute-start.26 = (bf16[512,512]{1,0:T(8,128)(2,1)S(1)}, bf16[512,512]{1,0:T(8,128)(2,1)S(1)}, u32[]{:S(2)}, u32[]{:S(2)}) collective-permute-start(bf16[512,512]{1,0:T(8,128)(2,1)S(1)} %get-tuple-element.22), channel_id=1, source_target_pairs={{0,16},{16,0},{1,17},{17,1},{2,18},{18,2},{3,19},{19,3},{4,20},{20... | collective-permute-start | bytes 1572872 | tf_op jit(solution)/shard_map/ppermute | solution.py:19
  122.2 35.3 %collective-permute-start.32 = (bf16[512,512]{1,0:T(8,128)(2,1)S(1)}, bf16[512,512]{1,0:T(8,128)(2,1)S(1)}, u32[]{:S(2)}, u32[]{:S(2)}) collective-permute-start(bf16[512,512]{1,0:T(8,128)(2,1)S(1)} %get-tuple-element.23), channel_id=1, source_target_pairs={{0,16},{16,0},{1,17},{17,1},{2,18},{18,2},{3,19},{19,3},{4,20},{20... | collective-permute-start | bytes 1572872 | tf_op jit(solution)/shard_map/ppermute | solution.py:19
  123.0 21.7 %collective-permute-start.33 = (bf16[512,512]{1,0:T(8,128)(2,1)S(1)}, bf16[512,512]{1,0:T(8,128)(2,1)S(1)}, u32[]{:S(2)}, u32[]{:S(2)}) collective-permute-start(bf16[512,512]{1,0:T(8,128)(2,1)S(1)} %get-tuple-element.23), channel_id=1, source_target_pairs={{0,4},{12,8},{1,5},{13,9},{2,6},{14,10},{3,7},{15,11},{16,20},{28,... | collective-permute-start | bytes 1572872 | tf_op jit(solution)/shard_map/ppermute | solution.py:190
  126.6 32.2 %collective-permute-start.38 = (bf16[512,512]{1,0:T(8,128)(2,1)S(1)}, bf16[512,512]{1,0:T(8,128)(2,1)S(1)}, u32[]{:S(2)}, u32[]{:S(2)}) collective-permute-start(bf16[512,512]{1,0:T(8,128)(2,1)S(1)} %get-tuple-element.24), channel_id=1, source_target_pairs={{0,16},{16,0},{1,17},{17,1},{2,18},{18,2},{3,19},{19,3},{4,20},{20... | collective-permute-start | bytes 1572872 | tf_op jit(solution)/shard_map/ppermute | solution.py:19
  133.5 22.5 %collective-permute-start.39 = (bf16[512,512]{1,0:T(8,128)(2,1)S(1)}, bf16[512,512]{1,0:T(8,128)(2,1)S(1)}, u32[]{:S(2)}, u32[]{:S(2)}) collective-permute-start(bf16[512,512]{1,0:T(8,128)(2,1)S(1)} %get-tuple-element.24), channel_id=1, source_target_pairs={{0,4},{12,8},{1,5},{13,9},{2,6},{14,10},{3,7},{15,11},{16,20},{28,... | collective-permute-start | bytes 1572872 | tf_op jit(solution)/shard_map/ppermute | solution.py:190
  144.7 38.7 %collective-permute-start.21 = (bf16[256,1024]{1,0:T(8,128)(2,1)S(1)}, bf16[256,1024]{1,0:T(8,128)(2,1)S(1)}, u32[]{:S(2)}, u32[]{:S(2)}) collective-permute-start(bf16[256,1024]{1,0:T(8,128)(2,1)S(1)} %maximum_maximum_fusion.2), channel_id=1, source_target_pairs={{0,4},{12,8},{1,5},{13,9},{2,6},{14,10},{3,7},{15,11},{16,20},{28,... | collective-permute-start | bytes 1572872 | tf_op jit(solution)/shard_map/ppermute | solution.py:172
  149.2 29.0 %collective-permute-start.20 = (bf16[256,1024]{1,0:T(8,128)(2,1)S(1)}, bf16[256,1024]{1,0:T(8,128)(2,1)S(1)}, u32[]{:S(2)}, u32[]{:S(2)}) collective-permute-start(bf16[256,1024]{1,0:T(8,128)(2,1)S(1)} %maximum_maximum_fusion.1), channel_id=1, source_target_pairs={{0,4},{12,8},{1,5},{13,9},{2,6},{14,10},{3,7},{15,11},{16,20},{28,... | collective-permute-start | bytes 1572872 | tf_op jit(solution)/shard_map/ppermute | solution.py:172
  156.0 31.2 %collective-permute-start.7 = (bf16[128,4096]{1,0:T(8,128)(2,1)S(1)}, bf16[128,4096]{1,0:T(8,128)(2,1)S(1)}, u32[]{:S(2)}, u32[]{:S(2)}) collective-permute-start(bf16[128,4096]{1,0:T(8,128)(2,1)S(1)} %get-tuple-element.39), channel_id=1, source_target_pairs={{0,1},{1,0},{2,3},{3,2},{4,5},{5,4},{6,7},{7,6},{8,9},{9,8},{10,11... | collective-permute-start | bytes 3145736 | tf_op jit(solution)/shard_map/ppermute | solution.py:19
  157.5 47.0 %collective-permute-start.8 = (bf16[128,4096]{1,0:T(8,128)(2,1)S(1)}, bf16[128,4096]{1,0:T(8,128)(2,1)S(1)}, u32[]{:S(2)}, u32[]{:S(2)}) collective-permute-start(bf16[128,4096]{1,0:T(8,128)(2,1)S(1)} %get-tuple-element.41), channel_id=1, source_target_pairs={{0,2},{1,3},{2,0},{3,1},{4,6},{5,7},{6,4},{7,5},{8,10},{9,11},{10,... | collective-permute-start | bytes 3145736 | tf_op jit(solution)/shard_map/ppermute | solution.py:19
  158.9 45.6 %collective-permute-start.9 = (bf16[128,4096]{1,0:T(8,128)(2,1)S(1)}, bf16[128,4096]{1,0:T(8,128)(2,1)S(1)}, u32[]{:S(2)}, u32[]{:S(2)}) collective-permute-start(bf16[128,4096]{1,0:T(8,128)(2,1)S(1)} %get-tuple-element.40), channel_id=1, source_target_pairs={{0,3},{1,2},{2,1},{3,0},{4,7},{5,6},{6,5},{7,4},{8,11},{9,10},{10,... | collective-permute-start | bytes 3145736 | tf_op jit(solution)/shard_map/ppermute | solution.py:19
  178.2 29.7 %collective-permute-start.22 = (bf16[256,1024]{1,0:T(8,128)(2,1)S(1)}, bf16[256,1024]{1,0:T(8,128)(2,1)S(1)}, u32[]{:S(2)}, u32[]{:S(2)}) collective-permute-start(bf16[256,1024]{1,0:T(8,128)(2,1)S(1)} %maximum_maximum_fusion.3), channel_id=1, source_target_pairs={{0,4},{12,8},{1,5},{13,9},{2,6},{14,10},{3,7},{15,11},{16,20},{28,... | collective-permute-start | bytes 1572872 | tf_op jit(solution)/shard_map/ppermute | solution.py:172
  183.4 34.7 %collective-permute-start.16 = (bf16[1024,512]{1,0:T(8,128)(2,1)S(1)}, bf16[1024,512]{1,0:T(8,128)(2,1)S(1)}, u32[]{:S(2)}, u32[]{:S(2)}) collective-permute-start(bf16[1024,512]{1,0:T(8,128)(2,1)S(1)} %constant_dynamic-slice_fusion.16), channel_id=1, source_target_pairs={{0,4},{12,8},{1,5},{13,9},{2,6},{14,10},{3,7},{15,11},{16,20},{28,... | collective-permute-start | bytes 3145736 | tf_op jit(solution)/shard_map/ppermute | solution.py:179
  187.1 21.8 %collective-permute-start.18 = (bf16[512,512]{1,0:T(8,128)(2,1)}, bf16[512,512]{1,0:T(8,128)(2,1)S(1)}, u32[]{:S(2)}, u32[]{:S(2)}) collective-permute-start(bf16[512,512]{1,0:T(8,128)(2,1)} %collective-permute-done.17), channel_id=1, source_target_pairs={{0,16},{16,0},{1,17},{17,1},{2,18},{18,2},{3,19},{19,3},{4,20},{20... | collective-permute-start | bytes 1572872 | tf_op jit(solution)/shard_map/ppermute | solution.py:19
  209.0 122.7 %collective-permute-start.10 = (bf16[128,4096]{1,0:T(8,128)(2,1)}, bf16[128,4096]{1,0:T(8,128)(2,1)}, u32[]{:S(2)}, u32[]{:S(2)}) collective-permute-start(bf16[128,4096]{1,0:T(8,128)(2,1)} %add_convert_fusion.1), channel_id=1, source_target_pairs={{0,16},{16,0},{1,17},{17,1},{2,18},{18,2},{3,19},{19,3},{4,20},{20... | collective-permute-start | bytes 3145736 | tf_op jit(solution)/shard_map/ppermute | solution.py:19
  211.1 17.2 %collective-permute-start.23 = (bf16[512,512]{0,1:T(8,128)(2,1)S(1)}, bf16[512,512]{0,1:T(8,128)(2,1)S(1)}, u32[]{:S(2)}, u32[]{:S(2)}) collective-permute-start(bf16[512,512]{0,1:T(8,128)(2,1)S(1)} %fusion.17), channel_id=1, source_target_pairs={{4,8},{8,4},{5,9},{9,5},{6,10},{10,6},{7,11},{11,7},{20,24},{24,20... | collective-permute-start | bytes 1572872 | tf_op jit(solution)/shard_map/ppermute | solution.py:197
  214.9 74.9 %collective-permute-start.29 = (bf16[512,512]{0,1:T(8,128)(2,1)S(1)}, bf16[512,512]{0,1:T(8,128)(2,1)S(1)}, u32[]{:S(2)}, u32[]{:S(2)}) collective-permute-start(bf16[512,512]{0,1:T(8,128)(2,1)S(1)} %fusion.20), channel_id=1, source_target_pairs={{4,8},{8,4},{5,9},{9,5},{6,10},{10,6},{7,11},{11,7},{20,24},{24,20... | collective-permute-start | bytes 1572872 | tf_op jit(solution)/shard_map/ppermute | solution.py:197
  224.8 62.0 %collective-permute-start.25 = (bf16[512,512]{0,1:T(8,128)(2,1)S(1)}, bf16[512,512]{0,1:T(8,128)(2,1)S(1)}, u32[]{:S(2)}, u32[]{:S(2)}) collective-permute-start(bf16[512,512]{0,1:T(8,128)(2,1)S(1)} %fusion.18), channel_id=1, source_target_pairs={{4,0},{8,12},{5,1},{9,13},{6,2},{10,14},{7,3},{11,15},{20,16},{24,... | collective-permute-start | bytes 1572872 | tf_op jit(solution)/shard_map/ppermute | solution.py:199
  226.9 79.4 %collective-permute-start.35 = (bf16[512,512]{0,1:T(8,128)(2,1)S(1)}, bf16[512,512]{0,1:T(8,128)(2,1)S(1)}, u32[]{:S(2)}, u32[]{:S(2)}) collective-permute-start(bf16[512,512]{0,1:T(8,128)(2,1)S(1)} %fusion.23), channel_id=1, source_target_pairs={{4,8},{8,4},{5,9},{9,5},{6,10},{10,6},{7,11},{11,7},{20,24},{24,20... | collective-permute-start | bytes 1572872 | tf_op jit(solution)/shard_map/ppermute | solution.py:197
  228.4 75.5 %collective-permute-start.31 = (bf16[512,512]{0,1:T(8,128)(2,1)S(1)}, bf16[512,512]{0,1:T(8,128)(2,1)S(1)}, u32[]{:S(2)}, u32[]{:S(2)}) collective-permute-start(bf16[512,512]{0,1:T(8,128)(2,1)S(1)} %fusion.21), channel_id=1, source_target_pairs={{4,0},{8,12},{5,1},{9,13},{6,2},{10,14},{7,3},{11,15},{20,16},{24,... | collective-permute-start | bytes 1572872 | tf_op jit(solution)/shard_map/ppermute | solution.py:199
  286.8 28.3 %collective-permute-start.37 = (bf16[512,512]{0,1:T(8,128)(2,1)S(1)}, bf16[512,512]{0,1:T(8,128)(2,1)S(1)}, u32[]{:S(2)}, u32[]{:S(2)}) collective-permute-start(bf16[512,512]{0,1:T(8,128)(2,1)S(1)} %fusion.24), channel_id=1, source_target_pairs={{4,0},{8,12},{5,1},{9,13},{6,2},{10,14},{7,3},{11,15},{20,16},{24,... | collective-permute-start | bytes 1572872 | tf_op jit(solution)/shard_map/ppermute | solution.py:199
  289.9 27.9 %collective-permute-start.41 = (bf16[512,512]{0,1:T(8,128)(2,1)S(1)}, bf16[512,512]{0,1:T(8,128)(2,1)S(1)}, u32[]{:S(2)}, u32[]{:S(2)}) collective-permute-start(bf16[512,512]{0,1:T(8,128)(2,1)S(1)} %fusion.26), channel_id=1, source_target_pairs={{4,8},{8,4},{5,9},{9,5},{6,10},{10,6},{7,11},{11,7},{20,24},{24,20... | collective-permute-start | bytes 1572872 | tf_op jit(solution)/shard_map/ppermute | solution.py:197
  303.9 20.6 %collective-permute-start.43 = (bf16[512,512]{0,1:T(8,128)(2,1)S(1)}, bf16[512,512]{0,1:T(8,128)(2,1)S(1)}, u32[]{:S(2)}, u32[]{:S(2)}) collective-permute-start(bf16[512,512]{0,1:T(8,128)(2,1)S(1)} %fusion.27), channel_id=1, source_target_pairs={{4,0},{8,12},{5,1},{9,13},{6,2},{10,14},{7,3},{11,15},{20,16},{24,... | collective-permute-start | bytes 1572872 | tf_op jit(solution)/shard_map/ppermute | solution.py:199
  (31 other events, 207.2 us)
